TPU v7x, 512 devices: a whole 4x4x16 slice. The times are simulated.
512 devices in a mesh: tm: 16 (over z_lo, x), ctx: 32 (over y, z_hi, core).
Axes of the slice: x: 4, y: 4, z: 16 (z_hi: 4, z_lo: 4; z = z_hi * 4 + z_lo), core: 2. Of those that a mesh axis runs over, the one named last changes fastest.
Arguments:
- states: float32 [16, 3072, 64], P('tm', 'ctx'), may hold values from -6 to 6
- noise_draws: float32 [16, 3072, 64], P('tm', 'ctx'), may hold values from -6 to 6
- plan: int32 [17], replicated, may hold values from 0 to 1000, as said below
- w_embed: bfloat16 [64, 3072], replicated, may hold values from -0.75 to 0.75
- w_time: bfloat16 [128, 3072], replicated, may hold values from -0.5 to 0.5
- w_query: bfloat16 [16, 3072, 128], P('tm'), may hold values from -0.109375 to 0.109375
- w_key: bfloat16 [16, 3072, 128], P('tm'), may hold values from -0.109375 to 0.109375
- w_value: bfloat16 [16, 3072, 128], P('tm'), may hold values from -0.109375 to 0.109375
- gain_query: float32 [16, 128], P('tm'), may hold values from 0.5 to 16, as said below
- gain_key: float32 [16, 128], P('tm'), may hold values from 0.5 to 16, as said below
- w_out: bfloat16 [16, 128, 3072], P('tm'), may hold values from -0.5 to 0.5
- w_final: bfloat16 [3072, 64], replicated, may hold values from -0.109375 to 0.109375
Outputs:
- new_states: float32 [16, 3072, 64], P('tm', 'ctx')
Inputs may be any that keep to these rules, and one draw needn't show every extreme that they name: plan[0] is 1000 and each later entry is smaller than the one before by 31 to 61. `gain_query`: positive gains. `gain_key`: positive gains.
All inputs are finite; a program needn't handle non-finite values.
Results may differ from a plain program's by a relative error of at most 0.014.
The roundings to bfloat16 on the way count: a program that leaves them out, or rounds other values in their place, can miss the bound.
Values may be sent and summed in bfloat16 or wider, within the bound.
No kernel may reach another device: no remote copies, remote signals or barrier semaphores. Data moves between devices by JAX's collectives and lax.ppermute only.
A program may use at most 64 MiB of HBM per device.

v0:
```python
import math
import jax
import jax.numpy as jnp
from jax import lax
from jax.sharding import PartitionSpec as P


def with_halo(array, sides, width):
    for axis, dim in sides:
        size, length = (lax.axis_size(axis), array.shape[dim])
        up = [(i, (i + 1) % size) for i in range(size - 1)]
        down = [(j, i) for i, j in up]
        last = lax.slice_in_dim(array, length - width, length, axis=dim)
        first = lax.slice_in_dim(array, 0, width, axis=dim)
        before = lax.ppermute(last, axis, up)
        after = lax.ppermute(first, axis, down)
        array = jnp.concatenate([before, array, after], axis=dim)
    return array


def entering(value, axis, join, neutral):
    count, mine = (lax.axis_size(axis), lax.axis_index(axis))
    pieces = lax.all_gather(value, axis)
    total = jnp.full_like(value, 0) + jnp.asarray(neutral, value.dtype)

    def hop(position, total):
        longer = join(total, pieces[position])
        return jnp.where(position < mine, longer, total)

    return lax.fori_loop(0, count - 1, hop, total)


def fourier_rows(plan, freq_count, step_count):
    half_freq = freq_count // 2
    frequency = jnp.exp(-math.log(10000.0) * jnp.arange(half_freq, dtype=jnp.float32) / half_freq)
    phase_arg = plan[:step_count].astype(jnp.float32)[:, None] * frequency[None, :]
    return jnp.concatenate([jnp.cos(phase_arg), jnp.sin(phase_arg)], axis=1).astype(jnp.bfloat16)


def rms_gain(values_in, gain_row):
    scale = lax.rsqrt(jnp.mean(values_in * values_in, axis=-1, keepdims=True) + 1e-06)
    return values_in * scale * gain_row


def per_device(
    states,
    noise_draws,
    plan,
    w_embed,
    w_time,
    w_query,
    w_key,
    w_value,
    gain_query,
    gain_key,
    w_out,
    w_final,
):
    every = lax.all_gather(states, "tm", axis=0, tiled=True)
    nsteps, tok_rows, channels = every.shape
    own_steps = states.shape[0]
    model_width = w_embed.shape[1]
    head_dim = w_query.shape[2]
    ctx_count = lax.axis_size("ctx")
    ctx_index = lax.axis_index("ctx")
    tm_index = lax.axis_index("tm")
    features = fourier_rows(plan, w_time.shape[0], nsteps)
    time_shift = jnp.dot(features, w_time, preferred_element_type=jnp.float32)
    latents = every.astype(jnp.bfloat16)
    count = latents.shape[1]
    embedded = jnp.dot(
        latents.reshape(nsteps * count, channels), w_embed, preferred_element_type=jnp.float32
    )
    hidden = (embedded.reshape(nsteps, count, model_width) + time_shift[:, None, :]).astype(
        jnp.bfloat16
    )
    count = hidden.shape[1]
    flat_rows = hidden.reshape(nsteps * count, model_width)
    key_rows = rms_gain(
        jnp.dot(flat_rows, w_key[0], preferred_element_type=jnp.float32), gain_key[0]
    ).astype(jnp.bfloat16)
    value_rows = jnp.dot(flat_rows, w_value[0], preferred_element_type=jnp.float32).astype(
        jnp.bfloat16
    )
    key_value = with_halo(
        jnp.concatenate([key_rows, value_rows], axis=1).reshape(nsteps, count, 2 * head_dim),
        (("ctx", 1),),
        tok_rows,
    )
    flat_hidden = hidden.reshape(nsteps * tok_rows, model_width)
    queries = rms_gain(
        jnp.dot(flat_hidden, w_query[0], preferred_element_type=jnp.float32), gain_query[0]
    ).astype(jnp.bfloat16)
    queries = queries.reshape(nsteps, tok_rows, head_dim)
    key_part = key_value[..., :head_dim]
    value_part = key_value[..., head_dim:]
    block_of = jnp.arange(3 * tok_rows, dtype=jnp.int32) // tok_rows
    valid = (
        (block_of == 1)
        | (block_of == 0) & (ctx_index > 0)
        | (block_of == 2) & (ctx_index < ctx_count - 1)
    )
    valid = valid[None, None, :]
    scores = jnp.einsum(
        "sqe,ske->sqk", queries, key_part, preferred_element_type=jnp.float32
    ) / math.sqrt(head_dim)
    top_score = jnp.max(jnp.where(valid, scores, -1e30), axis=-1, keepdims=True)
    expo = jnp.where(valid, jnp.exp(scores - top_score), 0.0)
    attn_probs = (expo / jnp.sum(expo, axis=-1, keepdims=True)).astype(jnp.bfloat16)
    attended = jnp.einsum(
        "sqk,ske->sqe", attn_probs, value_part, preferred_element_type=jnp.float32
    ).astype(jnp.bfloat16)
    projected = jnp.dot(
        attended.reshape(nsteps * tok_rows, head_dim), w_out[0], preferred_element_type=jnp.float32
    ).astype(jnp.bfloat16)
    head_terms = jnp.dot(projected, w_final, preferred_element_type=jnp.float32).reshape(
        nsteps, tok_rows, channels
    )
    own_hidden = lax.dynamic_slice_in_dim(hidden, tm_index * own_steps, own_steps, 0)
    residual = jnp.dot(
        own_hidden.reshape(own_steps * tok_rows, model_width),
        w_final,
        preferred_element_type=jnp.float32,
    )
    residual = residual.reshape(own_steps, tok_rows, channels)
    step_sizes = (plan[:-1] - plan[1:]).astype(jnp.float32) / 1000.0
    own_sizes = lax.dynamic_slice_in_dim(step_sizes, tm_index * own_steps, own_steps, 0)
    start_state = every[0][None, :, :]
    drift_rows = lax.psum_scatter(head_terms, "tm", scatter_dimension=0, tiled=True) + residual
    increment = (
        own_sizes[:, None, None] * drift_rows + jnp.sqrt(own_sizes)[:, None, None] * noise_draws
    )
    running = jnp.cumsum(increment, axis=0)
    earlier = entering(running[-1], "tm", jnp.add, jnp.zeros_like(running[-1]))
    return start_state + earlier[None, :, :] + running


def solution(mesh):
    return jax.shard_map(
        per_device,
        mesh=mesh,
        in_specs=(
            P("tm", "ctx", None),
            P("tm", "ctx", None),
            P(),
            P(),
            P(),
            P("tm", None, None),
            P("tm", None, None),
            P("tm", None, None),
            P("tm", None),
            P("tm", None),
            P("tm", None, None),
            P(),
        ),
        out_specs=P("tm", "ctx", None),
        check_vma=False,
    )
```

profile of v0, /device:TPU:8, one launch (start us, length us, event | category | flops | bytes accessed | tf_op | source)
XLA Modules:
  0.0 257.8 jit_solution(12405270481454556288)
XLA Ops:
  6.5 0.7 slice_convert_fusion
  7.3 46.7 %all_gather.6 = f32[16,96,64]{1,2,0:T(8,128)S(1)} all-gather(f32[1,96,64]{1,2,0:T(8,128)} %param.14), channel_id=1, replica_groups=mesh['tm'=16,'ctx'=32] {'tm'}, dimensions={0}, use_global_device_ids=true | all-gather | bytes 417792 | tf_op jit(solution)/shard_map/all_gather | solution.py:59
  54.0 0.1 fusion.27
  54.1 1.4 fusion.29
  55.5 3.9 %add_convert_fusion = bf16[16,96,3072]{2,1,0:T(8,128)(2,1)S(1)} fusion(f32[16,3072]{1,0:T(8,128)S(1)} %fusion.29, bf16[64,3072]{1,0:T(8,128)(2,1)} %param.17, f32[16,96,64]{1,2,0:T(8,128)S(1)} %all_gather.6), kind=kOutput, calls=%fused_computation.3 | convolution fusion | flops 613515264 | bytes 10420224 | tf_op jit(solution)/shard_map/dot_general | solution.py:71
  59.4 3.3 %multiply_reduce_fusion = (f32[1536]{0:T(1024)S(1)}, f32[1536,128]{0,1:T(8,128)S(1)}) fusion(bf16[1536,3072]{1,0:T(8,128)(2,1)S(1)} %bitcast.55, bf16[1,3072,128]{2,1,0:T(8,128)(2,1)S(1)} %copy-done), kind=kOutput, calls=%fused_computation.32 | convolution fusion | flops 1208351232 | bytes 11016192 | tf_op jit(solution)/shard_map/dot_general | solution.py:80
  62.7 0.3 copy-done.1
  63.0 3.3 %convolution_convert_fusion.1 = bf16[1536,128]{0,1:T(8,128)(2,1)S(1)} fusion(bf16[1536,3072]{1,0:T(8,128)(2,1)S(1)} %bitcast.56, bf16[1,3072,128]{2,1,0:T(8,128)(2,1)S(1)} %copy-done.2), kind=kOutput, calls=%fused_computation.6 | convolution fusion | flops 1208156160 | bytes 10616832 | tf_op jit(solution)/shard_map/dot_general | solution.py:82
  66.3 0.1 multiply_convert_fusion
  66.5 0.3 copy.22
  66.7 1.9 collective-permute-start
  68.7 8.6 %collective-permute-start.1 = (bf16[16,96,256]{2,1,0:T(8,128)(2,1)S(1)}, bf16[16,96,256]{2,1,0:T(8,128)(2,1)}, u32[]{:S(2)}, u32[]{:S(2)}) collective-permute-start(bf16[16,96,256]{2,1,0:T(8,128)(2,1)S(1)} %bitcast.59), channel_id=1, source_target_pairs={{1,0},{2,1},{3,2},{4,3},{5,4},{6,5},{7,6},{8,7},{9,8},{10,9},{11,1... | collective-permute-start | bytes 2359304 | tf_op jit(solution)/shard_map/ppermute | solution.py:16
  77.3 5.5 %multiply_reduce_fusion.1 = (f32[1536]{0:T(1024)S(1)}, f32[1536,128]{1,0:T(8,128)S(1)}) fusion(bf16[1536,3072]{1,0:T(8,128)(2,1)} %bitcast.57, bf16[1,3072,128]{2,1,0:T(8,128)(2,1)} %param.19), kind=kOutput, calls=%fused_computation.34 | convolution fusion | flops 1208351232 | bytes 11016192 | tf_op jit(solution)/shard_map/dot_general | solution.py:92
  82.9 0.3 multiply_convert_fusion.1
  83.2 24.8 %collective-permute-done = bf16[16,96,256]{2,1,0:T(8,128)(2,1)} collective-permute-done((bf16[16,96,256]{2,1,0:T(8,128)(2,1)S(1)}, bf16[16,96,256]{2,1,0:T(8,128)(2,1)}, u32[]{:S(2)}, u32[]{:S(2)}) %collective-permute-start) | collective-permute-done | bytes 786464 | tf_op jit(solution)/shard_map/ppermute | solution.py:15
  107.9 1.5 pad_maximum_fusion
  109.5 0.7 fusion.7
  110.2 1.0 fusion.40
  111.2 0.6 convolution_convert_fusion.2
  111.8 0.3 copy-done.3
  112.1 0.3 copy-done.7
  112.4 5.4 %fusion.1 = f32[1536,64]{0,1:T(8,128)S(1)} fusion(bf16[3072,64]{0,1:T(8,128)(2,1)S(1)} %copy-done.3, bf16[1536,128]{1,0:T(8,128)(2,1)S(1)} %bitcast.64, bf16[1,128,3072]{2,1,0:T(8,128)(2,1)S(1)} %copy-done.7), kind=kOutput, calls=%fused_computation.5 | convolution fusion | flops 1816657920 | bytes 1966080 | tf_op jit(solution)/shard_map/dot_general | solution.py:116
  117.8 0.2 reshape.81
  118.0 0.9 copy.23
  119.0 0.6 dynamic_slice.13
  120.2 85.3 %reduce-scatter.2.cloned.1.call-done = f32[1,96,64]{1,2,0:T(8,128)} async-done(((f32[16,96,64]{1,2,0:T(8,128)}), f32[1,96,64]{1,2,0:T(8,128)}) %reduce-scatter.2.cloned.1.call-update) | async-done | bytes 24592 | tf_op jit(solution)/shard_map/reduce_scatter | solution.py:129
  205.5 1.9 fusion.14
  207.5 40.5 %all_gather.7 = f32[16,96,64]{1,2,0:T(8,128)S(1)} all-gather(f32[1,96,64]{1,2,0:T(8,128)S(1)} %fusion.14), channel_id=1, replica_groups=mesh['tm'=16,'ctx'=32] {'tm'}, dimensions={0}, use_global_device_ids=true | all-gather | bytes 417792 | tf_op jit(solution)/shard_map/all_gather | solution.py:23
  248.0 2.2 while.14
  248.0 0.1 copy.28
  248.3 0.1 copy.28
  250.3 0.6 fusion.26
  (69 shorter events, 1.7 us)
Async XLA Ops:
  6.5 52.9 %copy-start = (bf16[1,3072,128]{2,1,0:T(8,128)(2,1)S(1)}, bf16[1,3072,128]{2,1,0:T(8,128)(2,1)}, u32[]{:S(2)}) copy-start(bf16[1,3072,128]{2,1,0:T(8,128)(2,1)} %param.20) | copy-start | bytes 2359300
  6.5 199.0 %reduce-scatter.2.cloned.1.call-start = ((), (), s32[]{:S(2)}) async-start(), calls=%async_computation.1 | async-start | bytes 557056 | tf_op jit(solution)/shard_map/reduce_scatter | solution.py:129
  59.4 3.6 %copy-start.1 = (bf16[16,96,3072]{2,1,0:T(8,128)(2,1)}, bf16[16,96,3072]{2,1,0:T(8,128)(2,1)S(1)}, u32[]{:S(2)}) copy-start(bf16[16,96,3072]{2,1,0:T(8,128)(2,1)S(1)} %add_convert_fusion) | copy-start | bytes 28311556
  59.4 3.6 %copy-start.2 = (bf16[1,3072,128]{2,1,0:T(8,128)(2,1)S(1)}, bf16[1,3072,128]{2,1,0:T(8,128)(2,1)}, u32[]{:S(2)}) copy-start(bf16[1,3072,128]{2,1,0:T(8,128)(2,1)} %param.21) | copy-start | bytes 2359300
  63.0 3.3 %copy-start.5 = (f32[1,128]{1,0:T(1,128)S(1)}, f32[1,128]{1,0:T(1,128)}, u32[]{:S(2)}) copy-start(f32[1,128]{1,0:T(1,128)} %param.23) | copy-start | bytes 1540
  66.7 41.2 %collective-permute-start = (bf16[16,96,256]{2,1,0:T(8,128)(2,1)S(1)}, bf16[16,96,256]{2,1,0:T(8,128)(2,1)}, u32[]{:S(2)}, u32[]{:S(2)}) collective-permute-start(bf16[16,96,256]{2,1,0:T(8,128)(2,1)S(1)} %bitcast.58), channel_id=1, source_target_pairs={{0,1},{1,2},{2,3},{3,4},{4,5},{5,6},{6,7},{7,8},{8,9},{9,10},{10,1... | collective-permute-start | bytes 2359304 | tf_op jit(solution)/shard_map/ppermute | solution.py:15
  68.7 39.3 %collective-permute-start.1 = (bf16[16,96,256]{2,1,0:T(8,128)(2,1)S(1)}, bf16[16,96,256]{2,1,0:T(8,128)(2,1)}, u32[]{:S(2)}, u32[]{:S(2)}) collective-permute-start(bf16[16,96,256]{2,1,0:T(8,128)(2,1)S(1)} %bitcast.59), channel_id=1, source_target_pairs={{1,0},{2,1},{3,2},{4,3},{5,4},{6,5},{7,6},{8,7},{9,8},{10,9},{11,1... | collective-permute-start | bytes 2359304 | tf_op jit(solution)/shard_map/ppermute | solution.py:16
  77.3 5.5 %copy-start.6 = (f32[1,128]{1,0:T(1,128)S(1)}, f32[1,128]{1,0:T(1,128)}, u32[]{:S(2)}) copy-start(f32[1,128]{1,0:T(1,128)} %param.22) | copy-start | bytes 1540
  111.1 1.0 copy-start.3
  111.2 1.2 copy-start.7
  117.8 1.2 copy-start.8
  117.8 87.8 %copy-start.4 = (f32[1,96,64]{1,2,0:T(8,128)S(1)}, f32[1,96,64]{1,2,0:T(8,128)}, u32[]{:S(2)}) copy-start(f32[1,96,64]{1,2,0:T(8,128)} %param.15) | copy-start | bytes 73732
Sparse Core Ops, SparseCore 0:
  119.1 86.4 reduce-scatter.1
where the time goes:
time: 258 us
  waiting for transfers between devices  110 us (43%)
  blocking collectives  87.3 us (34%)
  matrix products  25.9 us (10%)
  between operations  14.2 us (6%)
  starting transfers between devices  10.6 us (4%)
  other arithmetic  4.76 us (2%)
  local copies, waits for them, and re-layouts  4.32 us (2%)
    reduce_scatter x1, waiting for transfers between devices, per_device(): lax.psum_scatter(head_terms, 'tm', scatter_dimension=0, tiled=True)  85.3 us
    all_gather x1, blocking collectives, per_device(): every = lax.all_gather(states, 'tm', axis=0, tiled=True)  46.7 us
    all_gather x1, blocking collectives, entering(): pieces = lax.all_gather(value, axis)  40.5 us
    ppermute x1, waiting for transfers between devices, with_halo(): before = lax.ppermute(last, axis, up)  24.8 us
    ppermute x1, starting transfers between devices, with_halo(): after = lax.ppermute(first, axis, down)  8.63 us
    dot_general x1, matrix products, per_device(): jnp.dot(flat_hidden, w_query[0], preferred_element_type=jnp.float32)  5.49 us
    dot_general x1, matrix products, per_device(): jnp.dot(projected, w_final, preferred_element_type=jnp.float32)  5.35 us
  transfers between devices with their start and end apart: 3, of which 2 were waited for; matrix products, arithmetic and copies ran while one was open for 2% of the time, Pallas kernels for 0%

commit v1 on v0

--- a/solution.py
+++ b/solution.py
@@ -56,7 +56,9 @@
     w_out,
     w_final,
 ):
-    every = lax.all_gather(states, "tm", axis=0, tiled=True)
+    every = jnp.concatenate(
+        lax.all_to_all(jnp.stack([states] * lax.axis_size("tm")), "tm", 0, 0), axis=0
+    )
     nsteps, tok_rows, channels = every.shape
     own_steps = states.shape[0]
     model_width = w_embed.shape[1]

time: 258 us -> 241 us (0.934)
  the two profiles are of different devices: /device:TPU:8 before, /device:TPU:16 now
where the time goes in v1:
time: 241 us; the launch traced here: 240 us
  waiting for transfers between devices  131 us (54%)
  blocking collectives  40.5 us (17%)
  matrix products  24.9 us (10%)
  starting transfers between devices  19.1 us (8%)
  between operations  14.3 us (6%)
  local copies, waits for them, and re-layouts  6.09 us (3%)
  other arithmetic  3.32 us (1%)
    reduce_scatter x1, waiting for transfers between devices, per_device(): lax.psum_scatter(head_terms, 'tm', scatter_dimension=0, tiled=True)  89.5 us
    all_gather x1, blocking collectives, entering(): pieces = lax.all_gather(value, axis)  40.5 us
    ppermute x1, waiting for transfers between devices, with_halo(): after = lax.ppermute(first, axis, down)  22.3 us
    all_to_all x1, waiting for transfers between devices, per_device(): lax.all_to_all(jnp.stack([states] * lax.axis_size('tm')), 'tm', 0, 0)  13.2 us
    ppermute x1, starting transfers between devices, with_halo(): after = lax.ppermute(first, axis, down)  8.63 us
    all_to_all x1, starting transfers between devices, per_device(): lax.all_to_all(jnp.stack([states] * lax.axis_size('tm')), 'tm', 0, 0)  8.47 us
    ppermute x1, waiting for transfers between devices, with_halo(): before = lax.ppermute(last, axis, up)  6.55 us
    dot_general x1, matrix products, per_device(): jnp.dot(flat_hidden, w_query[0], preferred_element_type=jnp.float32)  5.48 us
  transfers between devices with their start and end apart: 4, of which 4 were waited for; matrix products, arithmetic and copies ran while one was open for 4% of the time, Pallas kernels for 0%

profile of v1, /device:TPU:16, one launch (start us, length us, event | category | flops | bytes accessed | tf_op | source)
XLA Modules:
  0.0 240.3 jit_solution(3448954836697229609)
XLA Ops:
  6.5 1.7 stack.2
  8.2 8.5 %all-to-all-start = ((f32[16,1,96,64]{2,3,1,0:T(8,128)}), f32[16,1,96,64]{2,3,1,0:T(8,128)S(1)}, u32[]{:S(2)}, u32[]{:S(2)}) async-start(f32[16,1,96,64]{2,3,1,0:T(8,128)} %stack.2), calls=%async_computation | async-start | bytes 1048576 | tf_op jit(solution)/shard_map/all_to_all | solution.py:60
  16.8 0.7 slice_convert_fusion
  17.6 1.4 fusion.32
  19.0 13.2 %all-to-all-done = f32[16,1,96,64]{2,3,1,0:T(8,128)S(1)} async-done(((f32[16,1,96,64]{2,3,1,0:T(8,128)}), f32[16,1,96,64]{2,3,1,0:T(8,128)S(1)}, u32[]{:S(2)}, u32[]{:S(2)}) %all-to-all-start) | async-done | bytes 393248 | tf_op jit(solution)/shard_map/all_to_all | solution.py:60
  32.2 2.8 %add_convert_fusion = bf16[16,96,3072]{2,1,0:T(8,128)(2,1)S(1)} fusion(f32[16,3072]{1,0:T(8,128)S(1)} %fusion.32, bf16[64,3072]{1,0:T(8,128)(2,1)S(1)} %copy-done.3, f32[16,1,96,64]{2,3,1,0:T(8,128)S(1)} %all-to-all-done), kind=kOutput, calls=%fused_computation.3 | convolution fusion | flops 613515264 | bytes 10420224 | tf_op jit(solution)/shard_map/dot_general | solution.py:73
  35.0 3.3 %multiply_reduce_fusion = (f32[1536]{0:T(1024)S(1)}, f32[1536,128]{0,1:T(8,128)S(1)}) fusion(bf16[1536,3072]{1,0:T(8,128)(2,1)S(1)} %bitcast.74, bf16[1,3072,128]{2,1,0:T(8,128)(2,1)S(1)} %copy-done), kind=kOutput, calls=%fused_computation.32 | convolution fusion | flops 1208351232 | bytes 11016192 | tf_op jit(solution)/shard_map/dot_general | solution.py:82
  38.3 0.3 copy-done.1
  38.6 3.3 %convolution_convert_fusion.1 = bf16[1536,128]{0,1:T(8,128)(2,1)S(1)} fusion(bf16[1536,3072]{1,0:T(8,128)(2,1)S(1)} %bitcast.75, bf16[1,3072,128]{2,1,0:T(8,128)(2,1)S(1)} %copy-done.2), kind=kOutput, calls=%fused_computation.6 | convolution fusion | flops 1208156160 | bytes 10616832 | tf_op jit(solution)/shard_map/dot_general | solution.py:84
  41.9 0.1 multiply_convert_fusion
  42.1 0.3 copy.23
  42.4 1.9 collective-permute-start
  44.3 8.6 %collective-permute-start.1 = (bf16[16,96,256]{2,1,0:T(8,128)(2,1)S(1)}, bf16[16,96,256]{2,1,0:T(8,128)(2,1)S(1)}, u32[]{:S(2)}, u32[]{:S(2)}) collective-permute-start(bf16[16,96,256]{2,1,0:T(8,128)(2,1)S(1)} %bitcast.78), channel_id=1, source_target_pairs={{1,0},{2,1},{3,2},{4,3},{5,4},{6,5},{7,6},{8,7},{9,8},{10,9},{11,1... | collective-permute-start | bytes 2359304 | tf_op jit(solution)/shard_map/ppermute | solution.py:16
  53.0 5.5 %multiply_reduce_fusion.1 = (f32[1536]{0:T(1024)S(1)}, f32[1536,128]{1,0:T(8,128)S(1)}) fusion(bf16[1536,3072]{1,0:T(8,128)(2,1)} %bitcast.76, bf16[1,3072,128]{2,1,0:T(8,128)(2,1)} %param.19), kind=kOutput, calls=%fused_computation.34 | convolution fusion | flops 1208351232 | bytes 11016192 | tf_op jit(solution)/shard_map/dot_general | solution.py:94
  58.5 0.3 multiply_convert_fusion.1
  58.7 6.5 %collective-permute-done = bf16[16,96,256]{2,1,0:T(8,128)(2,1)S(1)} collective-permute-done((bf16[16,96,256]{2,1,0:T(8,128)(2,1)S(1)}, bf16[16,96,256]{2,1,0:T(8,128)(2,1)S(1)}, u32[]{:S(2)}, u32[]{:S(2)}) %collective-permute-start) | collective-permute-done | bytes 786464 | tf_op jit(solution)/shard_map/ppermute | solution.py:15
  65.3 22.3 %collective-permute-done.1 = bf16[16,96,256]{2,1,0:T(8,128)(2,1)S(1)} collective-permute-done((bf16[16,96,256]{2,1,0:T(8,128)(2,1)S(1)}, bf16[16,96,256]{2,1,0:T(8,128)(2,1)S(1)}, u32[]{:S(2)}, u32[]{:S(2)}) %collective-permute-start.1) | collective-permute-done | bytes 786464 | tf_op jit(solution)/shard_map/ppermute | solution.py:16
  87.6 0.2 pad_maximum_fusion
  87.7 0.7 fusion.7
  88.4 1.0 fusion.43
  89.4 0.6 convolution_convert_fusion.2
  90.1 0.4 copy-done.4
  90.4 0.3 copy-done.8
  90.7 5.4 %fusion.1 = f32[1536,64]{0,1:T(8,128)S(1)} fusion(bf16[3072,64]{0,1:T(8,128)(2,1)S(1)} %copy-done.4, bf16[1536,128]{1,0:T(8,128)(2,1)S(1)} %bitcast.84, bf16[1,128,3072]{2,1,0:T(8,128)(2,1)S(1)} %copy-done.8), kind=kOutput, calls=%fused_computation.5 | convolution fusion | flops 1816657920 | bytes 1966080 | tf_op jit(solution)/shard_map/dot_general | solution.py:118
  96.0 0.2 reshape.90
  96.2 1.0 copy.24
  97.3 0.6 dynamic_slice.13
  98.6 89.5 %reduce-scatter.2.cloned.1.call-done = f32[1,96,64]{1,2,0:T(8,128)} async-done(((f32[16,96,64]{1,2,0:T(8,128)}), f32[1,96,64]{1,2,0:T(8,128)}) %reduce-scatter.2.cloned.1.call-update) | async-done | bytes 24592 | tf_op jit(solution)/shard_map/reduce_scatter | solution.py:131
  188.0 2.0 fusion.14
  190.0 40.5 %all_gather.3 = f32[16,96,64]{1,2,0:T(8,128)S(1)} all-gather(f32[1,96,64]{1,2,0:T(8,128)S(1)} %fusion.14), channel_id=1, replica_groups=mesh['tm'=16,'ctx'=32] {'tm'}, dimensions={0}, use_global_device_ids=true | all-gather | bytes 417792 | tf_op jit(solution)/shard_map/all_gather | solution.py:23
  230.5 2.2 while.14
  232.8 0.6 fusion.29
  (73 shorter events, 2.1 us)
Async XLA Ops:
  6.5 28.5 %copy-start = (bf16[1,3072,128]{2,1,0:T(8,128)(2,1)S(1)}, bf16[1,3072,128]{2,1,0:T(8,128)(2,1)}, u32[]{:S(2)}) copy-start(bf16[1,3072,128]{2,1,0:T(8,128)(2,1)} %param.20) | copy-start | bytes 2359300
  6.5 25.6 %copy-start.3 = (bf16[64,3072]{1,0:T(8,128)(2,1)S(1)}, bf16[64,3072]{1,0:T(8,128)(2,1)}, u32[]{:S(2)}) copy-start(bf16[64,3072]{1,0:T(8,128)(2,1)} %param.17) | copy-start | bytes 1179652
  8.2 23.9 %all-to-all-start = ((f32[16,1,96,64]{2,3,1,0:T(8,128)}), f32[16,1,96,64]{2,3,1,0:T(8,128)S(1)}, u32[]{:S(2)}, u32[]{:S(2)}) async-start(f32[16,1,96,64]{2,3,1,0:T(8,128)} %stack.2), calls=%async_computation | async-start | bytes 1048576 | tf_op jit(solution)/shard_map/all_to_all | solution.py:60
  16.7 171.3 %reduce-scatter.2.cloned.1.call-start = ((), (), s32[]{:S(2)}) async-start(), calls=%async_computation.2 | async-start | bytes 557056 | tf_op jit(solution)/shard_map/reduce_scatter | solution.py:131
  35.0 3.6 %copy-start.1 = (bf16[16,96,3072]{2,1,0:T(8,128)(2,1)}, bf16[16,96,3072]{2,1,0:T(8,128)(2,1)S(1)}, u32[]{:S(2)}) copy-start(bf16[16,96,3072]{2,1,0:T(8,128)(2,1)S(1)} %add_convert_fusion) | copy-start | bytes 28311556
  35.0 3.6 %copy-start.2 = (bf16[1,3072,128]{2,1,0:T(8,128)(2,1)S(1)}, bf16[1,3072,128]{2,1,0:T(8,128)(2,1)}, u32[]{:S(2)}) copy-start(bf16[1,3072,128]{2,1,0:T(8,128)(2,1)} %param.21) | copy-start | bytes 2359300
  38.6 3.3 %copy-start.6 = (f32[1,128]{1,0:T(1,128)S(1)}, f32[1,128]{1,0:T(1,128)}, u32[]{:S(2)}) copy-start(f32[1,128]{1,0:T(1,128)} %param.23) | copy-start | bytes 1540
  42.4 16.1 %copy-start.7 = (f32[1,128]{1,0:T(1,128)S(1)}, f32[1,128]{1,0:T(1,128)}, u32[]{:S(2)}) copy-start(f32[1,128]{1,0:T(1,128)} %param.22) | copy-start | bytes 1540
  42.4 22.9 %collective-permute-start = (bf16[16,96,256]{2,1,0:T(8,128)(2,1)S(1)}, bf16[16,96,256]{2,1,0:T(8,128)(2,1)S(1)}, u32[]{:S(2)}, u32[]{:S(2)}) collective-permute-start(bf16[16,96,256]{2,1,0:T(8,128)(2,1)S(1)} %bitcast.77), channel_id=1, source_target_pairs={{0,1},{1,2},{2,3},{3,4},{4,5},{5,6},{6,7},{7,8},{8,9},{9,10},{10,1... | collective-permute-start | bytes 2359304 | tf_op jit(solution)/shard_map/ppermute | solution.py:15
  44.3 43.3 %collective-permute-start.1 = (bf16[16,96,256]{2,1,0:T(8,128)(2,1)S(1)}, bf16[16,96,256]{2,1,0:T(8,128)(2,1)S(1)}, u32[]{:S(2)}, u32[]{:S(2)}) collective-permute-start(bf16[16,96,256]{2,1,0:T(8,128)(2,1)S(1)} %bitcast.78), channel_id=1, source_target_pairs={{1,0},{2,1},{3,2},{4,3},{5,4},{6,5},{7,6},{8,7},{9,8},{10,9},{11,1... | collective-permute-start | bytes 2359304 | tf_op jit(solution)/shard_map/ppermute | solution.py:16
  89.4 1.0 copy-start.4
  89.4 1.2 copy-start.8
  96.0 1.2 copy-start.9
  96.0 92.0 %copy-start.5 = (f32[1,96,64]{1,2,0:T(8,128)S(1)}, f32[1,96,64]{1,2,0:T(8,128)}, u32[]{:S(2)}) copy-start(f32[1,96,64]{1,2,0:T(8,128)} %param.15) | copy-start | bytes 73732
Sparse Core Ops, SparseCore 0:
  97.3 90.6 reduce-scatter.1
